TPU v7x, 32 devices: a whole 2x2x4 slice. The times are simulated.
32 devices in a mesh: groups: 2 (over y), op: 4 (over z), sec: 2 (over x), help: 2 (over core).
Axes of the slice: x: 2, y: 2, z: 4, core: 2. Of those that a mesh axis runs over, the one named last changes fastest.
Arguments:
- psi_one: bfloat16 [16, 256, 256], P(('groups', 'sec'), ('op', 'help')), parts along dimension 0, may hold values from -6 to 6
- psi_two: bfloat16 [16, 256, 256], P(('groups', 'sec'), ('op', 'help')), parts along dimension 0, may hold values from -6 to 6
- left_blocks: bfloat16 [64, 256, 256], P(('groups', 'op')), parts along dimension 0, may hold values from -0.375 to 0.375
- right_blocks: bfloat16 [64, 256, 256], P(('groups', 'op')), parts along dimension 0, may hold values from -0.046875 to 0.046875
- task_in: int32 [8, 2, 64], P(('groups', 'op'), 'sec'), parts along dimension 0, may hold values from 0 to 3
- task_out: int32 [8, 2, 64], P(('groups', 'op'), 'sec'), parts along dimension 0, may hold values from 0 to 3
- task_left: int32 [8, 2, 64], P(('groups', 'op'), 'sec'), parts along dimension 0, may hold values from 0 to 7
- task_right: int32 [8, 2, 64], P(('groups', 'op'), 'sec'), parts along dimension 0, may hold values from 0 to 7
- task_count: int32 [8, 2], P(('groups', 'op'), 'sec'), parts along dimension 0, may hold values from 16 to 64
Outputs:
- sigma_one: float32 [16, 256, 256], P(('groups', 'sec'), ('op', 'help')), parts along dimension 0
- sigma_two: float32 [16, 256, 256], P(('groups', 'sec'), ('op', 'help')), parts along dimension 0
- subspace: float32 [4, 2], P('groups'), parts along dimension 0
There are 2 independent parts, one for each index of `groups`. A program takes and returns all parts, laid end to end along the dimension named above; each array names one. Nothing has to cross between parts.
All inputs are finite; a program needn't handle non-finite values.
Results may differ from a plain program's by a relative error of at most 0.0029.
Values may be sent and summed in bfloat16 or wider, within the bound.
No kernel may reach another device: no remote copies, remote signals or barrier semaphores. Data moves between devices by JAX's collectives and lax.ppermute only.
A program may use at most 64 MiB of HBM per device.

v0:
```python
import math

import jax
import jax.numpy as jnp
from jax import lax
from jax.sharding import PartitionSpec as P


def local(
    psi_one,
    psi_two,
    left_blocks,
    right_blocks,
    task_in,
    task_out,
    task_left,
    task_right,
    task_count,
):
    gathered = (
        lax.all_gather(psi_one, ("op", "help"), axis=1, tiled=True),
        lax.all_gather(psi_two, ("op", "help"), axis=1, tiled=True),
    )
    waves = jnp.stack(gathered)
    sectors = psi_one.shape[0]
    width = psi_one.shape[2]
    slots = task_in.shape[-1]
    helpers = lax.axis_size("help")
    helper = lax.axis_index("help")
    live = task_count.reshape(())
    inputs = task_in.reshape(slots)
    targets = task_out.reshape(slots)
    lefts = task_left.reshape(slots)
    rights = task_right.reshape(slots)
    span = slots // helpers
    slot_ids = jnp.arange(slots, dtype=jnp.int32)
    first = helper * span
    stride = 1
    count = jnp.clip(live - first, 0, span)
    per_batch = min(8, span)
    local_ids = jnp.arange(sectors, dtype=jnp.int32)
    rounds = (count + per_batch - 1) // per_batch

    def one_round(turn, accum):
        position = turn * per_batch + jnp.arange(per_batch, dtype=jnp.int32)
        valid = position < count
        place = jnp.minimum(first + stride * position, slots - 1)
        slot = jnp.take(slot_ids, place)
        block = jnp.take(waves, jnp.take(inputs, slot), axis=1)
        left = jnp.take(left_blocks, jnp.take(lefts, slot), axis=0)
        right = jnp.take(right_blocks, jnp.take(rights, slot), axis=0)
        inner = jnp.einsum(
            "tij,vtjk->vtik", left, block, preferred_element_type=jnp.float32
        ).astype(jnp.bfloat16)
        contrib = jnp.einsum("vtik,tlk->vtil", inner, right, preferred_element_type=jnp.float32)
        onehot = ((jnp.take(targets, slot)[:, None] == local_ids[None, :]) & valid[:, None]).astype(
            jnp.float32
        )
        return accum + jnp.einsum("ts,vtab->vsab", onehot, contrib, precision=lax.Precision.HIGHEST)

    accum = lax.fori_loop(
        0, rounds, one_round, jnp.zeros((2, local_ids.shape[0], width, width), jnp.float32)
    )
    shares = lax.psum_scatter(accum, ("op", "help"), scatter_dimension=2, tiled=True)
    own_waves = jnp.stack([psi_one, psi_two]).astype(jnp.float32)
    dots = jnp.einsum("vsab,wsab->vw", own_waves, shares, precision=lax.Precision.HIGHEST)
    totals = lax.psum(dots, ("op", "sec", "help"))
    subspace = totals / math.sqrt(sectors * lax.axis_size("sec") * width * width)
    return (shares[0], shares[1], subspace)


def solution(mesh):
    placed = (
        P(("groups", "sec"), ("op", "help"), None),
        P(("groups", "sec"), ("op", "help"), None),
        P(("groups", "op"), None, None),
        P(("groups", "op"), None, None),
        P(("groups", "op"), "sec", None),
        P(("groups", "op"), "sec", None),
        P(("groups", "op"), "sec", None),
        P(("groups", "op"), "sec", None),
        P(("groups", "op"), "sec"),
    )
    return jax.shard_map(
        local,
        mesh=mesh,
        in_specs=placed,
        out_specs=(
            P(("groups", "sec"), ("op", "help"), None),
            P(("groups", "sec"), ("op", "help"), None),
            P("groups", None),
        ),
        check_vma=False,
    )
```

profile of v0, /device:TPU:0, one launch (start us, length us, event | category | flops | bytes accessed | tf_op | source)
XLA Modules:
  0.0 235.7 jit_solution(14614840947568481408)
XLA Ops:
  7.9 16.8 %all_gather.6 = bf16[4,256,256]{2,1,0:T(8,128)(2,1)S(1)} all-gather(bf16[4,32,256]{2,1,0:T(8,128)(2,1)} %param.15), channel_id=1, replica_groups=mesh['groups'=2,'op'=4,'sec'=2,'help'=2] {'op','help'}, dimensions={1}, use_global_device_ids=true | all-gather | bytes 589824 | tf_op jit(solution)/shard_map/all_gather | solution.py:21
  24.7 14.9 %all_gather.7 = bf16[4,256,256]{2,1,0:T(8,128)(2,1)S(1)} all-gather(bf16[4,32,256]{2,1,0:T(8,128)(2,1)} %param.16), channel_id=1, replica_groups=mesh['groups'=2,'op'=4,'sec'=2,'help'=2] {'op','help'}, dimensions={1}, use_global_device_ids=true | all-gather | bytes 589824 | tf_op jit(solution)/shard_map/all_gather | solution.py:22
  40.3 85.1 %while.11 = (s32[]{:T(128)}, f32[2,4,256,256]{3,1,2,0:T(4,128)S(1)}, s32[]{:T(128)}, s32[]{:T(128)}, s32[64]{0:T(128)S(1)}, /*index=5*/bf16[8,256,256]{2,1,0:T(8...) while((s32[]{:T(128)}, ...), condition=%wide.region_1.4_spmd.clone, body=%wide.region_0.3_spmd.clone.sunk | while | flops 1127749120 | bytes 33576584 | solution.py:61
  41.6 0.6 gather_fusion.2
  42.3 0.6 gather_fusion.3
  43.0 2.0 gather_fusion.4
  45.0 2.8 %gather_fusion.5 = bf16[8,256,256]{2,1,0:T(8,128)(2,1)} fusion(bf16[8,256,256]{2,1,0:T(8,128)(2,1)} %get-tuple-element.272, s32[1024]{0:T(1024)S(1)} %get-tuple-element.231), kind=kCustom, calls=%fused_computation.6.clone.clone.1 | custom fusion | bytes 2097184 | tf_op jit(solution)/shard_map/while/body/jit(_take)/gather | solution.py:50
  47.8 2.8 %gather_fusion.6 = bf16[8,256,256]{2,1,0:T(8,128)(2,1)} fusion(bf16[8,256,256]{2,1,0:T(8,128)(2,1)} %get-tuple-element.268, s32[1024]{0:T(1024)S(1)} %pad_clamp_fusion.12), kind=kCustom, calls=%fused_computation.1.clone.clone.1 | custom fusion | bytes 2097184 | tf_op jit(solution)/shard_map/while/body/jit(_take)/gather | solution.py:51
  50.7 5.6 %fusion.57 = f32[8,256,2,256]{3,1,2,0:T(8,128)} fusion(bf16[8,2,256,256]{3,2,1,0:T(8,128)(2,1)} %gather_fusion.4, pred[8]{0:T(512)(128)(4,1)S(1)} %get-tuple-element.230, bf16[8,256,256]{2,1,0:T(8,128)(2,1)} %gather_fusion.5, bf16[8,256,256]{2,1,0:T(8,128)(2,1)} %gather_fusion.6, pred[8]{0:T(512)(128)(4,1)S(1)} %get-tuple-element.233, ...), kind=kOutput, calls=%fused_computation.13.clone.1 | convolution fusion | flops 1076887552 | bytes 8388632 | tf_op jit(solution)/shard_map/while/body/vtik,tlk->vtil/dot_general | solution.py:55
  56.3 5.5 %copy.28 = f32[8,256,2,256]{1,0,3,2:T(8,128)} copy(f32[8,256,2,256]{3,1,2,0:T(8,128)} %fusion.57) | data formatting | bytes 8388608 | tf_op jit(solution)/shard_map/while/body/vtik,tlk->vtil/dot_general | solution.py:55
  62.5 6.2 %bitcast_add_fusion.2 = f32[2,4,256,256]{3,1,2,0:T(4,128)S(1)} fusion(f32[2,4,256,256]{3,1,2,0:T(4,128)S(1)} %get-tuple-element.250, f32[8,256,2,256]{1,0,3,2:T(8,128)} %copy.28, s32[8]{0:T(128)S(1)} %broadcast_select_fusion.2, pred[8]{0:T(512)(128)(4,1)S(1)} %fusion.58), kind=kOutput, calls=%fused_computation.12.clone.1 | convolution fusion | flops 50856000 | bytes 8388648 | tf_op jit(solution)/shard_map/while/body/ts,vtab->vsab/dot_general | solution.py:59
  70.0 0.6 gather_fusion.2
  70.7 0.6 gather_fusion.3
  71.3 2.0 gather_fusion.4
  73.4 2.8 %gather_fusion.5 = bf16[8,256,256]{2,1,0:T(8,128)(2,1)} fusion(bf16[8,256,256]{2,1,0:T(8,128)(2,1)} %get-tuple-element.272, s32[1024]{0:T(1024)S(1)} %get-tuple-element.231), kind=kCustom, calls=%fused_computation.6.clone.clone.1 | custom fusion | bytes 2097184 | tf_op jit(solution)/shard_map/while/body/jit(_take)/gather | solution.py:50
  76.2 2.8 %gather_fusion.6 = bf16[8,256,256]{2,1,0:T(8,128)(2,1)} fusion(bf16[8,256,256]{2,1,0:T(8,128)(2,1)} %get-tuple-element.268, s32[1024]{0:T(1024)S(1)} %pad_clamp_fusion.12), kind=kCustom, calls=%fused_computation.1.clone.clone.1 | custom fusion | bytes 2097184 | tf_op jit(solution)/shard_map/while/body/jit(_take)/gather | solution.py:51
  79.0 5.6 %fusion.57 = f32[8,256,2,256]{3,1,2,0:T(8,128)} fusion(bf16[8,2,256,256]{3,2,1,0:T(8,128)(2,1)} %gather_fusion.4, pred[8]{0:T(512)(128)(4,1)S(1)} %get-tuple-element.230, bf16[8,256,256]{2,1,0:T(8,128)(2,1)} %gather_fusion.5, bf16[8,256,256]{2,1,0:T(8,128)(2,1)} %gather_fusion.6, pred[8]{0:T(512)(128)(4,1)S(1)} %get-tuple-element.233, ...), kind=kOutput, calls=%fused_computation.13.clone.1 | convolution fusion | flops 1076887552 | bytes 8388632 | tf_op jit(solution)/shard_map/while/body/vtik,tlk->vtil/dot_general | solution.py:55
  84.6 5.5 %copy.28 = f32[8,256,2,256]{1,0,3,2:T(8,128)} copy(f32[8,256,2,256]{3,1,2,0:T(8,128)} %fusion.57) | data formatting | bytes 8388608 | tf_op jit(solution)/shard_map/while/body/vtik,tlk->vtil/dot_general | solution.py:55
  90.8 6.2 %bitcast_add_fusion.2 = f32[2,4,256,256]{3,1,2,0:T(4,128)S(1)} fusion(f32[2,4,256,256]{3,1,2,0:T(4,128)S(1)} %get-tuple-element.250, f32[8,256,2,256]{1,0,3,2:T(8,128)} %copy.28, s32[8]{0:T(128)S(1)} %broadcast_select_fusion.2, pred[8]{0:T(512)(128)(4,1)S(1)} %fusion.58), kind=kOutput, calls=%fused_computation.12.clone.1 | convolution fusion | flops 50856000 | bytes 8388648 | tf_op jit(solution)/shard_map/while/body/ts,vtab->vsab/dot_general | solution.py:59
  98.4 0.6 gather_fusion.2
  99.7 2.0 gather_fusion.4
  101.7 2.8 %gather_fusion.5 = bf16[8,256,256]{2,1,0:T(8,128)(2,1)} fusion(bf16[8,256,256]{2,1,0:T(8,128)(2,1)} %get-tuple-element.272, s32[1024]{0:T(1024)S(1)} %get-tuple-element.231), kind=kCustom, calls=%fused_computation.6.clone.clone.1 | custom fusion | bytes 2097184 | tf_op jit(solution)/shard_map/while/body/jit(_take)/gather | solution.py:50
  104.6 2.8 %gather_fusion.6 = bf16[8,256,256]{2,1,0:T(8,128)(2,1)} fusion(bf16[8,256,256]{2,1,0:T(8,128)(2,1)} %get-tuple-element.268, s32[1024]{0:T(1024)S(1)} %pad_clamp_fusion.12), kind=kCustom, calls=%fused_computation.1.clone.clone.1 | custom fusion | bytes 2097184 | tf_op jit(solution)/shard_map/while/body/jit(_take)/gather | solution.py:51
  107.4 5.6 %fusion.57 = f32[8,256,2,256]{3,1,2,0:T(8,128)} fusion(bf16[8,2,256,256]{3,2,1,0:T(8,128)(2,1)} %gather_fusion.4, pred[8]{0:T(512)(128)(4,1)S(1)} %get-tuple-element.230, bf16[8,256,256]{2,1,0:T(8,128)(2,1)} %gather_fusion.5, bf16[8,256,256]{2,1,0:T(8,128)(2,1)} %gather_fusion.6, pred[8]{0:T(512)(128)(4,1)S(1)} %get-tuple-element.233, ...), kind=kOutput, calls=%fused_computation.13.clone.1 | convolution fusion | flops 1076887552 | bytes 8388632 | tf_op jit(solution)/shard_map/while/body/vtik,tlk->vtil/dot_general | solution.py:55
  113.0 5.5 %copy.28 = f32[8,256,2,256]{1,0,3,2:T(8,128)} copy(f32[8,256,2,256]{3,1,2,0:T(8,128)} %fusion.57) | data formatting | bytes 8388608 | tf_op jit(solution)/shard_map/while/body/vtik,tlk->vtil/dot_general | solution.py:55
  119.2 6.2 %bitcast_add_fusion.2 = f32[2,4,256,256]{3,1,2,0:T(4,128)S(1)} fusion(f32[2,4,256,256]{3,1,2,0:T(4,128)S(1)} %get-tuple-element.250, f32[8,256,2,256]{1,0,3,2:T(8,128)} %copy.28, s32[8]{0:T(128)S(1)} %broadcast_select_fusion.2, pred[8]{0:T(512)(128)(4,1)S(1)} %fusion.58), kind=kOutput, calls=%fused_computation.12.clone.1 | convolution fusion | flops 50856000 | bytes 8388648 | tf_op jit(solution)/shard_map/while/body/ts,vtab->vsab/dot_general | solution.py:59
  125.4 1.8 copy.16
  127.2 0.8 copy-done.4
  128.2 64.6 %reduce-scatter.2.cloned.1.call-done = f32[2,4,32,256]{3,2,1,0:T(8,128)} async-done(((f32[2,4,256,256]{3,2,1,0:T(8,128)}), f32[2,4,32,256]{3,2,1,0:T(8,128)}) %reduce-scatter.2.cloned.1.call-update) | async-done | bytes 262160 | tf_op jit(solution)/shard_map/reduce_scatter | solution.py:64
  192.8 2.5 %convolution_bitcast_fusion = f32[2,2]{1,0:T(2,128)S(1)} fusion(f32[2,4,32,256]{3,2,1,0:T(8,128)} %reduce-scatter.2.cloned.1.call-done, bf16[1,4,32,256]{3,0,1,2:T(2,128)(2,1)S(1)} %copy.18, bf16[1,4,32,256]{3,0,1,2:T(2,128)(2,1)S(1)} %copy.17), kind=kOutput, calls=%fused_computation.52 | convolution fusion | flops 1835008 | bytes 393232 | tf_op jit(solution)/shard_map/vsab,wsab->vw/dot_general | solution.py:66
  195.3 31.3 %psum.7 = f32[2,2]{1,0:T(2,128)S(1)} all-reduce(f32[2,2]{1,0:T(2,128)S(1)} %convolution_bitcast_fusion), channel_id=1, replica_groups=mesh['groups'=2,'op'=4,'sec'=2,'help'=2] {'op','sec','help'}, use_global_device_ids=true, to_apply=%region_3.6 | all-reduce | flops 4 | bytes 32 | tf_op jit(solution)/shard_map/psum | solution.py:67
  227.2 1.7 slice_bitcast_fusion
  (58 shorter events, 8.2 us)
Async XLA Ops:
  7.2 185.7 %reduce-scatter.2.cloned.1.call-start = ((), (), s32[]{:S(2)}) async-start(), calls=%async_computation.1 | async-start | bytes 2359296 | tf_op jit(solution)/shard_map/reduce_scatter | solution.py:64
  39.6 0.7 copy-start
  39.6 0.7 copy-start.1
  39.6 0.7 copy-start.2
  39.6 0.7 copy-start.3
  127.1 0.8 copy-start.4
  127.1 0.9 copy-start.5
Sparse Core Ops, SparseCore 0:
  127.3 65.4 reduce-scatter.1
where the time goes:
time: 237 us; the launch traced here: 236 us
  waiting for transfers between devices  64.6 us (27%)
  blocking collectives  63 us (27%)
  local copies, waits for them, and re-layouts  54.4 us (23%)
  matrix products  37.8 us (16%)
  between operations  14.7 us (6%)
    reduce_scatter x1, waiting for transfers between devices, local(): lax.psum_scatter(accum, ('op', 'help'), scatter_dimension=2, tiled=True)  64.6 us
    psum x1, blocking collectives, local(): totals = lax.psum(dots, ('op', 'sec', 'help'))  31.3 us
    dot_general x3, matrix products, one_round(): jnp.einsum('ts,vtab->vsab', onehot, contrib, precision=lax.Precision.HIGH...  18.5 us
    dot_general x3, matrix products, one_round(): jnp.einsum('vtik,tlk->vtil', inner, right, preferred_element_type=jnp.flo...  16.8 us
    all_gather x1, blocking collectives, local(): lax.all_gather(psi_one, ('op', 'help'), axis=1, tiled=True)  16.8 us
    dot_general x3, local copies, waits for them, and re-layouts, one_round(): jnp.einsum('vtik,tlk->vtil', inner, right, preferred_element_type=jnp.flo...  16.6 us
    all_gather x1, blocking collectives, local(): lax.all_gather(psi_two, ('op', 'help'), axis=1, tiled=True)  14.9 us
    gather x6, local copies, waits for them, and re-layouts, one_round(): right = jnp.take(right_blocks, jnp.take(rights, slot), axis=0)  10.4 us
  transfers between devices with their start and end apart: 1, of which 1 were waited for; matrix products, arithmetic and copies ran while one was open for 0% of the time, Pallas kernels for 0%

commit v1 on v0

v1 whole, which is shorter than its diff:
```python
import functools
import math

import jax
import jax.numpy as jnp
from jax import lax
from jax.experimental import pallas as pl
from jax.experimental.pallas import tpu as pltpu
from jax.sharding import PartitionSpec as P

GROUP = 4
F32 = jnp.float32
BF16 = jnp.bfloat16
SMEM = pltpu.SMEM
VMEM = pltpu.VMEM


def plan_kernel(sectors, ops, slots, inputs, targets, lefts, rights, count, block_ref, right_ref, starts_ref):
    live = count[0]
    spare = sectors * ops

    def tally(t, tallies):
        here = jnp.where(t < live, targets[t], sectors)
        return tuple(n + jnp.where(here == c, 1, 0) for c, n in enumerate(tallies))

    tallies = lax.fori_loop(0, slots, tally, tuple(jnp.int32(0) for _ in range(sectors)))
    first = jnp.int32(0)
    begins = []
    for c in range(sectors):
        begins.append(first)
        starts_ref[c] = first // GROUP
        padded = (tallies[c] + GROUP - 1) // GROUP * GROUP
        for i in range(GROUP):
            block_ref[first + tallies[c] + i] = spare
            right_ref[first + tallies[c] + i] = 0
        first = first + padded
    starts_ref[sectors] = first // GROUP

    def place(t, cursors):
        here = targets[t]
        at = jnp.int32(0)
        for c in range(sectors):
            at = jnp.where(here == c, cursors[c], at)
        block_ref[at] = inputs[t] * ops + lefts[t]
        right_ref[at] = rights[t]
        return tuple(n + jnp.where(here == c, 1, 0) for c, n in enumerate(cursors))

    lax.fori_loop(0, live, place, tuple(begins))


def make_plan(sectors, ops, slots, tasks, count):
    room = slots + 2 * sectors * GROUP + GROUP
    spec = pl.BlockSpec(memory_space=SMEM)
    return pl.pallas_call(
        functools.partial(plan_kernel, sectors, ops, slots),
        out_shape=(
            jax.ShapeDtypeStruct((room,), jnp.int32),
            jax.ShapeDtypeStruct((room,), jnp.int32),
            jax.ShapeDtypeStruct((sectors + 1,), jnp.int32),
        ),
        in_specs=[spec] * 5,
        out_specs=(spec,) * 3,
        name="plan",
    )(*tasks, count)


def tile_of(x):
    total = None
    for r in range(0, x.shape[0], 8):
        for c in range(0, x.shape[1], 128):
            part = x[r : r + 8, c : c + 128]
            total = part if total is None else total + part
    return total


def product_kernel(n_op, in_place, place, block, right, starts, left_ref, right_ref, *refs):
    n_in = 2 * n_op if in_place else 1
    waves_in, refs = refs[:n_in], refs[n_in:]
    n_out = n_op if in_place else 1
    outs, (dots_ref, waves, inner, sums) = refs[:n_out], refs[n_out:]
    _, sectors, width, _ = waves.shape
    ops = left_ref.shape[0]
    half = left_ref.shape[1] * left_ref.shape[2]
    rows = left_ref.shape[2]
    me, helper = place[0], place[1]
    if in_place:
        for k in range(n_op):
            origin = lax.rem(me - k + n_op, n_op)
            for other in range(2):
                owner = helper if other == 0 else 1 - helper
                at = pl.multiple_of((origin * 2 + owner) * rows, rows)
                waves[:, :, pl.ds(at, rows), :] = waves_in[other * n_op + k][...]
    else:
        waves[...] = waves_in[0][...]
    left = left_ref[...].reshape(ops * half, width)
    for a in range(sectors):
        for v in range(2):
            found = jnp.dot(left, waves[v, a], preferred_element_type=F32).astype(BF16)
            inner[pl.ds(a * ops, ops), v] = found.reshape(ops, half, width)
    inner[sectors * ops] = jnp.zeros((2, half, width), BF16)
    sums[...] = jnp.zeros_like(sums)
    for c in range(sectors):

        def step(g, carry, c=c):
            total = sums[c]
            for i in range(GROUP):
                total = total + lax.dot_general(
                    inner[block[g * GROUP + i]].reshape(2 * half, width),
                    right_ref[right[g * GROUP + i]],
                    (((1,), (1,)), ((), ())),
                    preferred_element_type=F32,
                ).reshape(2, n_op, rows, width)
            sums[c] = total
            return carry

        lax.fori_loop(starts[c], starts[c + 1], step, 0)
    dots = [[None, None], [None, None]]
    for c in range(sectors):
        for origin in range(n_op):
            at = pl.multiple_of((origin * 2 + helper) * rows, rows)
            for v in range(2):
                wave = waves[v, c, pl.ds(at, rows), :].astype(F32)
                for w in range(2):
                    part = tile_of(wave * sums[c, w, origin])
                    dots[v][w] = part if dots[v][w] is None else dots[v][w] + part
    row = lax.broadcasted_iota(jnp.int32, (8, 128), 0)
    lane = lax.broadcasted_iota(jnp.int32, (8, 128), 1)
    tile = jnp.zeros((8, 128), F32)
    for v in range(2):
        for w in range(2):
            tile = jnp.where((row == v) & (lane == w), jnp.sum(dots[v][w]), tile)
    dots_ref[...] = tile
    if in_place:
        for k in range(n_op):
            goal = lax.rem(me + k, n_op)
            for c in range(sectors):
                for v in range(2):
                    outs[k][v, c] = sums[c, v, goal].astype(outs[k].dtype)
    else:
        outs[0][...] = sums[...]


def products(n_op, in_place, place, plan, left_blocks, right_blocks, waves, sectors, rows):
    ops, width, _ = right_blocks.shape
    half = n_op * rows
    if in_place:
        outs = [jax.ShapeDtypeStruct((2, sectors, rows, width), F32 if k == 0 else BF16) for k in range(n_op)]
    else:
        outs = [jax.ShapeDtypeStruct((sectors, 2, n_op, rows, width), F32)]
    outs.append(jax.ShapeDtypeStruct((8, 128), F32))

    left_spec = pl.BlockSpec((ops, n_op, None, rows, width), lambda i, place, *_: (0, 0, place[1], 0, 0))
    full = lambda s: pl.BlockSpec(s, lambda i, *_: (0,) * len(s))
    grid_spec = pltpu.PrefetchScalarGridSpec(
        num_scalar_prefetch=4,
        grid=(1,),
        in_specs=[left_spec, full(right_blocks.shape)] + [full(w.shape) for w in waves],
        out_specs=[full(o.shape) for o in outs],
        scratch_shapes=[
            pltpu.VMEM((2, sectors, width, width), BF16),
            pltpu.VMEM((sectors * ops + 1, 2, half, width), BF16),
            pltpu.VMEM((sectors, 2, n_op, rows, width), F32),
        ],
    )
    return pl.pallas_call(
        functools.partial(product_kernel, n_op, in_place),
        out_shape=outs,
        grid_spec=grid_spec,
        compiler_params=pltpu.CompilerParams(vmem_limit_bytes=48 * 1024 * 1024),
        name="products",
    )(place, *plan, left_blocks, right_blocks, *waves)


def finish_kernel(scale, n, own_ref, dots_ref, *refs):
    others, (one_ref, two_ref, subspace_ref) = refs[:n], refs[n:]
    for v, out in enumerate((one_ref, two_ref)):
        total = own_ref[v]
        for other in others:
            total = total + other[v].astype(F32)
        out[...] = total
    subspace_ref[...] = dots_ref[:2, :2] * scale


def finish(scale, own, others, dots):
    _, sectors, rows, width = own.shape
    whole = pl.BlockSpec(memory_space=VMEM)
    out = jax.ShapeDtypeStruct((sectors, rows, width), F32)
    return pl.pallas_call(
        functools.partial(finish_kernel, scale, len(others)),
        out_shape=(out, out, jax.ShapeDtypeStruct((2, 2), F32)),
        in_specs=[whole] * (2 + len(others)),
        out_specs=(whole,) * 3,
        name="finish",
    )(own, dots, *others)


def sum_over(x, axis):
    size = lax.axis_size(axis)
    if size & (size - 1):
        return lax.psum(x, axis)
    hop = 1
    while hop < size:
        x = x + lax.ppermute(x, axis, [(i, i ^ hop) for i in range(size)])
        hop *= 2
    return x


def local(
    psi_one,
    psi_two,
    left_blocks,
    right_blocks,
    task_in,
    task_out,
    task_left,
    task_right,
    task_count,
):
    sectors, rows, width = psi_one.shape
    ops = left_blocks.shape[0]
    slots = task_in.shape[-1]
    n_op = lax.axis_size("op")
    me = lax.axis_index("op")
    helper = lax.axis_index("help")
    in_place = rows % 16 == 0
    place = jnp.stack([me, helper]).astype(jnp.int32)
    tasks = [t.reshape(slots) for t in (task_in, task_out, task_left, task_right)]
    plan = make_plan(sectors, ops, slots, tasks, task_count.reshape(1))
    shift = lambda x, k: lax.ppermute(x, "op", [(i, (i + k) % n_op) for i in range(n_op)])
    swap = lambda x: lax.ppermute(x, "help", [(0, 1), (1, 0)])
    own = jnp.stack([psi_one, psi_two])
    if in_place:
        near = [own] + [shift(own, k) for k in range(1, n_op)]
        waves = near + [swap(x) for x in near]
    else:
        waves = [lax.all_gather(own, ("op", "help"), axis=2, tiled=True)]
    lefts = left_blocks.reshape(ops, n_op, 2, rows, width)
    *parts, dots = products(n_op, in_place, place, plan, lefts, right_blocks, waves, sectors, rows)
    if not in_place:
        sums = jnp.moveaxis(parts[0], 2, 0).swapaxes(1, 2)
        picked = [jnp.take(sums, (me + k) % n_op, axis=0) for k in range(n_op)]
        parts = [p if k == 0 else p.astype(BF16) for k, p in enumerate(picked)]
    others = [shift(parts[k], k) for k in range(1, n_op)]
    for axis in ("help", "sec", "op"):
        dots = sum_over(dots, axis)
    scale = 1.0 / math.sqrt(sectors * lax.axis_size("sec") * width * width)
    return finish(scale, parts[0], others, dots)


def solution(mesh):
    placed = (
        P(("groups", "sec"), ("op", "help"), None),
        P(("groups", "sec"), ("op", "help"), None),
        P(("groups", "op"), None, None),
        P(("groups", "op"), None, None),
        P(("groups", "op"), "sec", None),
        P(("groups", "op"), "sec", None),
        P(("groups", "op"), "sec", None),
        P(("groups", "op"), "sec", None),
        P(("groups", "op"), "sec"),
    )
    return jax.shard_map(
        local,
        mesh=mesh,
        in_specs=placed,
        out_specs=(
            P(("groups", "sec"), ("op", "help"), None),
            P(("groups", "sec"), ("op", "help"), None),
            P("groups", None),
        ),
        check_vma=False,
    )
```

time: 237 us -> 54.7 us (0.23)
  blocking collectives: 63 us -> 0 us
  local copies, waits for them, and re-layouts: 54.4 us -> 4.54 us
  waiting for transfers between devices: 64.6 us -> 20.3 us
  matrix products: 37.8 us -> 0 us
  between operations: 14.7 us -> 1.39 us
  starting transfers between devices: 0.04 us -> 13.3 us
  Pallas kernels: 0 us -> 12.8 us
    reduce_scatter x1 -> x0, waiting for transfers between devices: 64.6 us -> none  [local(): lax.psum_scatter(accum, ('op', 'help'), scatter_dimension=2, tiled=True)]
    dot_general x7 -> x0, matrix products: 37.8 us -> none  [the longest x3 18.5 us: one_round(): jnp.einsum('ts,vtab->vsab', onehot, contrib, precision=lax.Precision.HIGH...]
    gather x24 -> x0, local copies, waits for them, and re-layouts: 32.7 us -> none  [the longest x6 10.4 us: one_round(): right = jnp.take(right_blocks, jnp.take(rights, slot), axis=0)]
    all_gather x2 -> x0, blocking collectives: 31.7 us -> none  [the longest x1 16.8 us: local(): lax.all_gather(psi_one, ('op', 'help'), axis=1, tiled=True)]
    psum x1 -> x0, blocking collectives: 31.3 us -> none  [local(): totals = lax.psum(dots, ('op', 'sec', 'help'))]
    ppermute x0 -> x14, waiting for transfers between devices: none -> 20.3 us  [the longest x6 10.2 us: local(): lax.ppermute(x, 'op', [(i, (i + k) % n_op) for i in range(n_op)])]
    dot_general x3 -> x0, local copies, waits for them, and re-layouts: 16.6 us -> none  [one_round(): jnp.einsum('vtik,tlk->vtil', inner, right, preferred_element_type=jnp.flo...]
    ppermute x0 -> x14, starting transfers between devices: none -> 13.3 us  [the longest x6 9.94 us: local(): lax.ppermute(x, 'op', [(i, (i + k) % n_op) for i in range(n_op)])]
  transfers between devices with their start and end apart: 1 -> 14, of which waited for: 1 -> 6; matrix products, arithmetic and copies ran while one was open for 0% -> 1% of each run, Pallas kernels for 0% -> 6%
where the time goes in v1:
time: 54.7 us; the launch traced here: 53.9 us
  waiting for transfers between devices  20.3 us (37%)
  starting transfers between devices  13.3 us (24%)
  Pallas kernels  12.8 us (23%)
  local copies, waits for them, and re-layouts  4.54 us (8%)
  other arithmetic  1.57 us (3%)
  between operations  1.39 us (3%)
    ppermute x6, waiting for transfers between devices, local(): lax.ppermute(x, 'op', [(i, (i + k) % n_op) for i in range(n_op)])  10.2 us
    ppermute x4, waiting for transfers between devices, sum_over(): x = x + lax.ppermute(x, axis, [(i, i ^ hop) for i in range(size)])  10.1 us
    ppermute x6, starting transfers between devices, local(): lax.ppermute(x, 'op', [(i, (i + k) % n_op) for i in range(n_op)])  9.94 us
    pallas_call x1, Pallas kernels, products(): pl.pallas_call(functools.partial(product_kernel, n_op, in_place), out_sha...  7.92 us
    unnamed x18, local copies, waits for them, and re-layouts  4.54 us
    pallas_call x1, Pallas kernels, make_plan(): pl.pallas_call(functools.partial(plan_kernel, sectors, ops, slots), out_s...  3.03 us
    ppermute x4, starting transfers between devices, sum_over(): x = x + lax.ppermute(x, axis, [(i, i ^ hop) for i in range(size)])  2.85 us
    pallas_call x1, Pallas kernels, finish(): pl.pallas_call(functools.partial(finish_kernel, scale, len(others)), out_...  1.85 us
  transfers between devices with their start and end apart: 14, of which 6 were waited for; matrix products, arithmetic and copies ran while one was open for 1% of the time, Pallas kernels for 6%

profile of v1, /device:TPU:0, one launch (start us, length us, event | category | flops | bytes accessed | tf_op | source)
XLA Modules:
  0.0 53.9 jit_solution(7092129944649243385)
XLA Ops:
  0.6 0.9 %pad_maximum_fusion.refs_0_ = bf16[2,4,32,256]{3,2,1,0:T(8,128)(2,1)S(1)} fusion(bf16[1,4,32,256]{3,2,1,0:T(8,128)(2,1)} %bitcast.12, bf16[1,4,32,256]{3,2,1,0:T(8,128)(2,1)} %bitcast.13), kind=kLoop, calls=%fused_computation | loop fusion | flops 65536 | bytes 262144 | tf_op jit(solution)/shard_map/stack | solution.py:231
  1.5 5.1 %collective-permute-start.2 = (bf16[2,4,32,256]{3,2,1,0:T(8,128)(2,1)S(1)}, bf16[2,4,32,256]{3,2,1,0:T(8,128)(2,1)S(1)}, u32[]{:S(2)}, u32[]{:S(2)}) collective-permute-start(bf16[2,4,32,256]{3,2,1,0:T(8,128)(2,1)S(1)} %pad_maximum_fusion.refs_0_), channel_id=1, source_target_pairs={{0,12},{4,0},{8,4},{12,8},{1,13},{5,1},{9,5},{13,9},{2,14},{6,2},{... | collective-permute-start | bytes 393224 | tf_op jit(solution)/shard_map/ppermute | solution.py:229
  6.6 1.0 %collective-permute-start = (bf16[2,4,32,256]{3,2,1,0:T(8,128)(2,1)S(1)}, bf16[2,4,32,256]{3,2,1,0:T(8,128)(2,1)S(1)}, u32[]{:S(2)}, u32[]{:S(2)}) collective-permute-start(bf16[2,4,32,256]{3,2,1,0:T(8,128)(2,1)S(1)} %pad_maximum_fusion.refs_0_), channel_id=1, source_target_pairs={{0,4},{4,8},{8,12},{12,0},{1,5},{5,9},{9,13},{13,1},{2,6},{6,10},{... | collective-permute-start | bytes 393224 | tf_op jit(solution)/shard_map/ppermute | solution.py:229
  7.6 0.0 collective-permute-start.3
  7.6 2.9 %collective-permute-done.2.refs_3_ = bf16[2,4,32,256]{3,2,1,0:T(8,128)(2,1)S(1)} collective-permute-done((bf16[2,4,32,256]{3,2,1,0:T(8,128)(2,1)S(1)}, bf16[2,4,32,256]{3,2,1,0:T(8,128)(2,1)S(1)}, u32[]{:S(2)}, u32[]{:S(2)}) %collective-permute-start.2) | collective-permute-done | bytes 131104 | tf_op jit(solution)/shard_map/ppermute | solution.py:229
  10.5 0.0 collective-permute-start.6
  10.5 7.3 %collective-permute-done.1.refs_2_ = bf16[2,4,32,256]{3,2,1,0:T(8,128)(2,1)S(1)} collective-permute-done((bf16[2,4,32,256]{3,2,1,0:T(8,128)(2,1)S(1)}, bf16[2,4,32,256]{3,2,1,0:T(8,128)(2,1)S(1)}, u32[]{:S(2)}, u32[]{:S(2)}) %collective-permute-start.1) | collective-permute-done | bytes 131104 | tf_op jit(solution)/shard_map/ppermute | solution.py:229
  17.8 0.5 collective-permute-start.4
  19.0 3.0 %plan.1 = (s32[100]{0:T(128)}, s32[100]{0:T(128)}, s32[5]{0:T(128)}) custom-call(s32[64]{0:T(128)} %bitcast.14, s32[64]{0:T(128)} %bitcast.15, s32[64]{0:T(128)} %bitcast.16, s32[64]{0:T(128)} %bitcast.17, s32[1]{0:T(128)} %bitcast.10.count), custom_call_target="tpu_custom_call" | custom-call | tf_op jit(solution)/shard_map/plan/pallas_call | solution.py:54
  22.0 0.1 pad_add_fusion.place
  22.1 0.0 collective-permute-done.3.refs_4_
  22.1 0.0 collective-permute-done.6.refs_7_
  22.1 0.0 collective-permute-done.5.refs_6_
  22.2 0.6 %copy-done.3 = s32[100]{0:T(128)S(1)} copy-done((s32[100]{0:T(128)S(1)}, s32[100]{0:T(128)}, u32[]{:S(2)}) %copy-start.3) | copy-done | bytes 424
  22.7 0.1 copy-done.4
  22.8 1.2 %copy-done = bf16[8,256,256]{2,1,0:T(8,128)(2,1)S(1)} copy-done((bf16[8,256,256]{2,1,0:T(8,128)(2,1)S(1)}, bf16[8,256,256]{2,1,0:T(8,128)(2,1)}, u32[]{:S(2)}) %copy-start) | copy-done | bytes 1048600
  24.1 1.2 %copy-done.1 = bf16[8,256,256]{2,1,0:T(8,128)(2,1)S(1)} copy-done((bf16[8,256,256]{2,1,0:T(8,128)(2,1)S(1)}, bf16[8,256,256]{2,1,0:T(8,128)(2,1)}, u32[]{:S(2)}) %copy-start.1) | copy-done | bytes 1048600
  25.3 7.9 %products.1 = (f32[2,4,32,256]{3,2,1,0:T(8,128)S(1)}, bf16[2,4,32,256]{3,2,1,0:T(8,128)(2,1)S(1)}, bf16[2,4,32,256]{3,2,1,0:T(8,128)(2,1)S(1)}, bf16[2,4,32,256]{3,2,1,0:T(8,128)(2,1)S(1)}, f32[8,128]{1,0:T(8,128)S(1)}) custom-call(s32[2]{0:T(128)S(1)} %pad_add_fusion.place, s32[100]{0:T(128)S(1)} %copy-done.3, s32[100]{0:T(128)S(1)} %copy-done.4, ...), custom_call_target="tpu_custom_call" | custom-call | tf_op jit(solution)/shard_map/products/pallas_call | solution.py:165
  33.2 0.7 %copy-done.2 = f32[2,4,32,256]{3,2,1,0:T(8,128)} copy-done((f32[2,4,32,256]{3,2,1,0:T(8,128)}, f32[2,4,32,256]{3,2,1,0:T(8,128)S(1)}, u32[]{:S(2)}) %copy-start.2) | copy-done | bytes 262168
  33.9 3.8 %collective-permute-start.13 = (bf16[2,4,32,256]{3,2,1,0:T(8,128)(2,1)S(1)}, bf16[2,4,32,256]{3,2,1,0:T(8,128)(2,1)S(1)}, u32[]{:S(2)}, u32[]{:S(2)}) collective-permute-start(bf16[2,4,32,256]{3,2,1,0:T(8,128)(2,1)S(1)} %get-tuple-element.18), channel_id=1, source_target_pairs={{0,12},{4,0},{8,4},{12,8},{1,13},{5,1},{9,5},{13,9},{2,14},{6,2},{... | collective-permute-start | bytes 393224 | tf_op jit(solution)/shard_map/ppermute | solution.py:229
  37.8 1.2 %collective-permute-done.7 = f32[8,128]{1,0:T(8,128)S(1)} collective-permute-done((f32[8,128]{1,0:T(8,128)S(1)}, f32[8,128]{1,0:T(8,128)S(1)}, u32[]{:S(2)}, u32[]{:S(2)}) %collective-permute-start.7) | collective-permute-done | bytes 4128 | tf_op jit(solution)/shard_map/ppermute | solution.py:203
  38.9 0.3 collective-permute-start.8
  39.2 3.3 %collective-permute-done.8 = f32[8,128]{1,0:T(8,128)S(1)} collective-permute-done((f32[8,128]{1,0:T(8,128)S(1)}, f32[8,128]{1,0:T(8,128)S(1)}, u32[]{:S(2)}, u32[]{:S(2)}) %collective-permute-start.8) | collective-permute-done | bytes 4128 | tf_op jit(solution)/shard_map/ppermute | solution.py:203
  42.5 0.6 %collective-permute-start.9 = (f32[8,128]{1,0:T(8,128)S(1)}, f32[8,128]{1,0:T(8,128)S(1)}, u32[]{:S(2)}, u32[]{:S(2)}) collective-permute-start(f32[8,128]{1,0:T(8,128)S(1)} %add.13), channel_id=1, source_target_pairs={{0,4},{4,0},{8,12},{12,8},{1,5},{5,1},{9,13},{13,9},{2,6},{6,2},{1... | collective-permute-start | bytes 12296 | tf_op jit(solution)/shard_map/ppermute | solution.py:203
  43.1 3.1 %collective-permute-done.9 = f32[8,128]{1,0:T(8,128)S(1)} collective-permute-done((f32[8,128]{1,0:T(8,128)S(1)}, f32[8,128]{1,0:T(8,128)S(1)}, u32[]{:S(2)}, u32[]{:S(2)}) %collective-permute-start.9) | collective-permute-done | bytes 4128 | tf_op jit(solution)/shard_map/ppermute | solution.py:203
  46.2 2.0 %collective-permute-start.10 = (f32[8,128]{1,0:T(8,128)S(1)}, f32[8,128]{1,0:T(8,128)S(1)}, u32[]{:S(2)}, u32[]{:S(2)}) collective-permute-start(f32[8,128]{1,0:T(8,128)S(1)} %add.14), channel_id=1, source_target_pairs={{0,8},{4,12},{8,0},{12,4},{1,9},{5,13},{9,1},{13,5},{2,10},{6,14},... | collective-permute-start | bytes 12296 | tf_op jit(solution)/shard_map/ppermute | solution.py:203
  48.2 2.5 %collective-permute-done.10 = f32[8,128]{1,0:T(8,128)S(1)} collective-permute-done((f32[8,128]{1,0:T(8,128)S(1)}, f32[8,128]{1,0:T(8,128)S(1)}, u32[]{:S(2)}, u32[]{:S(2)}) %collective-permute-start.10) | collective-permute-done | bytes 4128 | tf_op jit(solution)/shard_map/ppermute | solution.py:203
  50.7 0.6 %add.15.dots_ref = f32[8,128]{1,0:T(8,128)} add(f32[8,128]{1,0:T(8,128)S(1)} %add.14, f32[8,128]{1,0:T(8,128)S(1)} %collective-permute-done.10) | non-fusion elementwise | flops 1024 | bytes 12288 | tf_op jit(solution)/shard_map/add | solution.py:203
  51.3 0.6 %copy-done.6 = bf16[2,4,32,256]{3,2,1,0:T(8,128)(2,1)} copy-done((bf16[2,4,32,256]{3,2,1,0:T(8,128)(2,1)}, bf16[2,4,32,256]{3,2,1,0:T(8,128)(2,1)S(1)}, u32[]{:S(2)}) %copy-start.6) | copy-done | bytes 131096
  51.9 0.1 copy-done.7
  52.0 0.0 copy-done.8
  52.0 1.9 %finish.1 = (f32[4,32,256]{2,1,0:T(8,128)}, f32[4,32,256]{2,1,0:T(8,128)}, f32[2,2]{1,0:T(2,128)}) custom-call(f32[2,4,32,256]{3,2,1,0:T(8,128)} %copy-done.2, f32[8,128]{1,0:T(8,128)} %add.15.dots_ref, bf16[2,4,32,256]{3,2,1,0:T(8,128)(2,1)} %copy-done.6, bf16[2,4,32,256]{3,2,1,0:T(8,128)(2,1)} %copy-done.7, bf16[2,4,32,256]{3,2,1,0:T(8,128)(2,1)} %copy-done.8), custom_call_target="tpu_custom_call" | custom-call | tf_op jit(solution)/shard_map/finish/pallas_call | solution.py:188
  (23 shorter events, 0.1 us)
Async XLA Ops:
  1.5 9.0 %collective-permute-start.2 = (bf16[2,4,32,256]{3,2,1,0:T(8,128)(2,1)S(1)}, bf16[2,4,32,256]{3,2,1,0:T(8,128)(2,1)S(1)}, u32[]{:S(2)}, u32[]{:S(2)}) collective-permute-start(bf16[2,4,32,256]{3,2,1,0:T(8,128)(2,1)S(1)} %pad_maximum_fusion.refs_0_), channel_id=1, source_target_pairs={{0,12},{4,0},{8,4},{12,8},{1,13},{5,1},{9,5},{13,9},{2,14},{6,2},{... | collective-permute-start | bytes 393224 | tf_op jit(solution)/shard_map/ppermute | solution.py:229
  6.6 11.2 %collective-permute-start.1 = (bf16[2,4,32,256]{3,2,1,0:T(8,128)(2,1)S(1)}, bf16[2,4,32,256]{3,2,1,0:T(8,128)(2,1)S(1)}, u32[]{:S(2)}, u32[]{:S(2)}) collective-permute-start(bf16[2,4,32,256]{3,2,1,0:T(8,128)(2,1)S(1)} %pad_maximum_fusion.refs_0_), channel_id=1, source_target_pairs={{0,8},{4,12},{8,0},{12,4},{1,9},{5,13},{9,1},{13,5},{2,10},{6,14},... | collective-permute-start | bytes 393224 | tf_op jit(solution)/shard_map/ppermute | solution.py:229
  6.6 11.2 %collective-permute-start = (bf16[2,4,32,256]{3,2,1,0:T(8,128)(2,1)S(1)}, bf16[2,4,32,256]{3,2,1,0:T(8,128)(2,1)S(1)}, u32[]{:S(2)}, u32[]{:S(2)}) collective-permute-start(bf16[2,4,32,256]{3,2,1,0:T(8,128)(2,1)S(1)} %pad_maximum_fusion.refs_0_), channel_id=1, source_target_pairs={{0,4},{4,8},{8,12},{12,0},{1,5},{5,9},{9,13},{13,1},{2,6},{6,10},{... | collective-permute-start | bytes 393224 | tf_op jit(solution)/shard_map/ppermute | solution.py:229
  7.6 14.5 %collective-permute-start.3 = (bf16[2,4,32,256]{3,2,1,0:T(8,128)(2,1)S(1)}, bf16[2,4,32,256]{3,2,1,0:T(8,128)(2,1)S(1)}, u32[]{:S(2)}, u32[]{:S(2)}) collective-permute-start(bf16[2,4,32,256]{3,2,1,0:T(8,128)(2,1)S(1)} %pad_maximum_fusion.refs_0_), channel_id=1, source_target_pairs={{0,1},{1,0},{2,3},{3,2},{4,5},{5,4},{6,7},{7,6},{8,9},{9,8},{10,11... | collective-permute-start | bytes 393224 | tf_op jit(solution)/shard_map/ppermute | solution.py:230
  10.5 11.6 %collective-permute-start.6 = (bf16[2,4,32,256]{3,2,1,0:T(8,128)(2,1)S(1)}, bf16[2,4,32,256]{3,2,1,0:T(8,128)(2,1)S(1)}, u32[]{:S(2)}, u32[]{:S(2)}) collective-permute-start(bf16[2,4,32,256]{3,2,1,0:T(8,128)(2,1)S(1)} %collective-permute-done.2.refs_3_), channel_id=1, source_target_pairs={{0,1},{1,0},{2,3},{3,2},{4,5},{5,4},{6,7},{7,6},{8,9},{9,8},{10,11... | collective-permute-start | bytes 393224 | tf_op jit(solution)/shard_map/ppermute | solution.py:230
  17.8 4.3 %collective-permute-start.5 = (bf16[2,4,32,256]{3,2,1,0:T(8,128)(2,1)S(1)}, bf16[2,4,32,256]{3,2,1,0:T(8,128)(2,1)S(1)}, u32[]{:S(2)}, u32[]{:S(2)}) collective-permute-start(bf16[2,4,32,256]{3,2,1,0:T(8,128)(2,1)S(1)} %collective-permute-done.1.refs_2_), channel_id=1, source_target_pairs={{0,1},{1,0},{2,3},{3,2},{4,5},{5,4},{6,7},{7,6},{8,9},{9,8},{10,11... | collective-permute-start | bytes 393224 | tf_op jit(solution)/shard_map/ppermute | solution.py:230
  17.8 4.3 %collective-permute-start.4 = (bf16[2,4,32,256]{3,2,1,0:T(8,128)(2,1)S(1)}, bf16[2,4,32,256]{3,2,1,0:T(8,128)(2,1)S(1)}, u32[]{:S(2)}, u32[]{:S(2)}) collective-permute-start(bf16[2,4,32,256]{3,2,1,0:T(8,128)(2,1)S(1)} %collective-permute-done.refs_1_), channel_id=1, source_target_pairs={{0,1},{1,0},{2,3},{3,2},{4,5},{5,4},{6,7},{7,6},{8,9},{9,8},{10,11... | collective-permute-start | bytes 393224 | tf_op jit(solution)/shard_map/ppermute | solution.py:230
  22.1 0.6 %copy-start.3 = (s32[100]{0:T(128)S(1)}, s32[100]{0:T(128)}, u32[]{:S(2)}) copy-start(s32[100]{0:T(128)} %get-tuple-element.11.block) | copy-start | bytes 1204
  22.1 0.7 %copy-start.4 = (s32[100]{0:T(128)S(1)}, s32[100]{0:T(128)}, u32[]{:S(2)}) copy-start(s32[100]{0:T(128)} %get-tuple-element.12.right) | copy-start | bytes 1204
  22.1 0.7 %copy-start.5 = (s32[5]{0:T(128)S(1)}, s32[5]{0:T(128)}, u32[]{:S(2)}) copy-start(s32[5]{0:T(128)} %get-tuple-element.13.starts) | copy-start | bytes 64
  22.8 1.2 %copy-start = (bf16[8,256,256]{2,1,0:T(8,128)(2,1)S(1)}, bf16[8,256,256]{2,1,0:T(8,128)(2,1)}, u32[]{:S(2)}) copy-start(bf16[8,256,256]{2,1,0:T(8,128)(2,1)} %param.11) | copy-start | bytes 3145732
  24.1 1.2 %copy-start.1 = (bf16[8,256,256]{2,1,0:T(8,128)(2,1)S(1)}, bf16[8,256,256]{2,1,0:T(8,128)(2,1)}, u32[]{:S(2)}) copy-start(bf16[8,256,256]{2,1,0:T(8,128)(2,1)} %right_ref.1) | copy-start | bytes 3145732
  33.2 0.7 %copy-start.2 = (f32[2,4,32,256]{3,2,1,0:T(8,128)}, f32[2,4,32,256]{3,2,1,0:T(8,128)S(1)}, u32[]{:S(2)}) copy-start(f32[2,4,32,256]{3,2,1,0:T(8,128)S(1)} %get-tuple-element.14.own_ref) | copy-start | bytes 786436
  33.9 17.4 %collective-permute-start.11 = (bf16[2,4,32,256]{3,2,1,0:T(8,128)(2,1)S(1)}, bf16[2,4,32,256]{3,2,1,0:T(8,128)(2,1)S(1)}, u32[]{:S(2)}, u32[]{:S(2)}) collective-permute-start(bf16[2,4,32,256]{3,2,1,0:T(8,128)(2,1)S(1)} %get-tuple-element.16), channel_id=1, source_target_pairs={{0,4},{4,8},{8,12},{12,0},{1,5},{5,9},{9,13},{13,1},{2,6},{6,10},{... | collective-permute-start | bytes 393224 | tf_op jit(solution)/shard_map/ppermute | solution.py:229
  33.9 17.4 %collective-permute-start.12 = (bf16[2,4,32,256]{3,2,1,0:T(8,128)(2,1)S(1)}, bf16[2,4,32,256]{3,2,1,0:T(8,128)(2,1)S(1)}, u32[]{:S(2)}, u32[]{:S(2)}) collective-permute-start(bf16[2,4,32,256]{3,2,1,0:T(8,128)(2,1)S(1)} %get-tuple-element.17), channel_id=1, source_target_pairs={{0,8},{4,12},{8,0},{12,4},{1,9},{5,13},{9,1},{13,5},{2,10},{6,14},... | collective-permute-start | bytes 393224 | tf_op jit(solution)/shard_map/ppermute | solution.py:229
  33.9 17.4 %collective-permute-start.13 = (bf16[2,4,32,256]{3,2,1,0:T(8,128)(2,1)S(1)}, bf16[2,4,32,256]{3,2,1,0:T(8,128)(2,1)S(1)}, u32[]{:S(2)}, u32[]{:S(2)}) collective-permute-start(bf16[2,4,32,256]{3,2,1,0:T(8,128)(2,1)S(1)} %get-tuple-element.18), channel_id=1, source_target_pairs={{0,12},{4,0},{8,4},{12,8},{1,13},{5,1},{9,5},{13,9},{2,14},{6,2},{... | collective-permute-start | bytes 393224 | tf_op jit(solution)/shard_map/ppermute | solution.py:229
  37.7 1.2 %collective-permute-start.7 = (f32[8,128]{1,0:T(8,128)S(1)}, f32[8,128]{1,0:T(8,128)S(1)}, u32[]{:S(2)}, u32[]{:S(2)}) collective-permute-start(f32[8,128]{1,0:T(8,128)S(1)} %get-tuple-element.15), channel_id=1, source_target_pairs={{0,1},{1,0},{2,3},{3,2},{4,5},{5,4},{6,7},{7,6},{8,9},{9,8},{10,11... | collective-permute-start | bytes 12296 | tf_op jit(solution)/shard_map/ppermute | solution.py:203
  38.9 3.6 %collective-permute-start.8 = (f32[8,128]{1,0:T(8,128)S(1)}, f32[8,128]{1,0:T(8,128)S(1)}, u32[]{:S(2)}, u32[]{:S(2)}) collective-permute-start(f32[8,128]{1,0:T(8,128)S(1)} %add.12), channel_id=1, source_target_pairs={{0,2},{2,0},{1,3},{3,1},{4,6},{6,4},{5,7},{7,5},{8,10},{10,8},{9,1... | collective-permute-start | bytes 12296 | tf_op jit(solution)/shard_map/ppermute | solution.py:203
  42.5 3.7 %collective-permute-start.9 = (f32[8,128]{1,0:T(8,128)S(1)}, f32[8,128]{1,0:T(8,128)S(1)}, u32[]{:S(2)}, u32[]{:S(2)}) collective-permute-start(f32[8,128]{1,0:T(8,128)S(1)} %add.13), channel_id=1, source_target_pairs={{0,4},{4,0},{8,12},{12,8},{1,5},{5,1},{9,13},{13,9},{2,6},{6,2},{1... | collective-permute-start | bytes 12296 | tf_op jit(solution)/shard_map/ppermute | solution.py:203
  46.2 4.5 %collective-permute-start.10 = (f32[8,128]{1,0:T(8,128)S(1)}, f32[8,128]{1,0:T(8,128)S(1)}, u32[]{:S(2)}, u32[]{:S(2)}) collective-permute-start(f32[8,128]{1,0:T(8,128)S(1)} %add.14), channel_id=1, source_target_pairs={{0,8},{4,12},{8,0},{12,4},{1,9},{5,13},{9,1},{13,5},{2,10},{6,14},... | collective-permute-start | bytes 12296 | tf_op jit(solution)/shard_map/ppermute | solution.py:203
  51.3 0.7 %copy-start.6 = (bf16[2,4,32,256]{3,2,1,0:T(8,128)(2,1)}, bf16[2,4,32,256]{3,2,1,0:T(8,128)(2,1)S(1)}, u32[]{:S(2)}) copy-start(bf16[2,4,32,256]{3,2,1,0:T(8,128)(2,1)S(1)} %collective-permute-done.11.refs_0_) | copy-start | bytes 393220
  51.3 0.7 %copy-start.7 = (bf16[2,4,32,256]{3,2,1,0:T(8,128)(2,1)}, bf16[2,4,32,256]{3,2,1,0:T(8,128)(2,1)S(1)}, u32[]{:S(2)}) copy-start(bf16[2,4,32,256]{3,2,1,0:T(8,128)(2,1)S(1)} %collective-permute-done.12.refs_1_) | copy-start | bytes 393220
  51.3 0.7 %copy-start.8 = (bf16[2,4,32,256]{3,2,1,0:T(8,128)(2,1)}, bf16[2,4,32,256]{3,2,1,0:T(8,128)(2,1)S(1)}, u32[]{:S(2)}) copy-start(bf16[2,4,32,256]{3,2,1,0:T(8,128)(2,1)S(1)} %collective-permute-done.13.refs_2_) | copy-start | bytes 393220
